TPU v7x, 32 devices: a whole 2x2x4 slice. The times are simulated.
32 devices in a mesh: pipe: 4 (over y, core), expert: 8 (over z, x).
Axes of the slice: x: 2, y: 2, z: 4, core: 2. Of those that a mesh axis runs over, the one named last changes fastest.
Arguments:
- grad_in: bfloat16 [4, 512, 2048], P('pipe', 'expert'), may hold values from -6 to 6
- head_grad: bfloat16 [512, 2048], P('expert'), may hold values from -6 to 6
- router_logits: float32 [4, 2, 512, 8], P('pipe', None, 'expert'), may hold values from -8 to 304
- route_ids: int32 [4, 2, 512, 2], P('pipe', None, 'expert'), may hold values from 0 to 7, all different within a row; in each aligned block of 64 rows (0 to 63, 64 to 127, ..., all dimensions but the last counted through in order) at most 24 rows name the same one
- gate_act: bfloat16 [4, 2, 6144, 192], P('pipe', None, 'expert'), may hold values from -6 to 6
- up_act: bfloat16 [4, 2, 6144, 192], P('pipe', None, 'expert'), may hold values from -6 to 6
- router_weight: bfloat16 [4, 2048, 8], P('pipe'), may hold values from -0.125 to 0.125
- gate_weight: bfloat16 [4, 6144, 2048], P('pipe', 'expert'), may hold values from -0.125 to 0.125
- up_weight: bfloat16 [4, 6144, 2048], P('pipe', 'expert'), may hold values from -0.125 to 0.125
- down_weight: bfloat16 [4, 6144, 2048], P('pipe', 'expert'), may hold values from -0.21875 to 0.21875
- z_weight: float32 [], replicated, may hold values from 0.5 to 2
Outputs:
- grad_out: bfloat16 [4, 512, 2048], P('pipe', 'expert')
- down_grad: bfloat16 [4, 6144, 2048], P('pipe', 'expert')
Inputs may be any that keep to these rules, and one draw needn't show every extreme that they name: `route_ids`: each row names 2 different experts. Within the 64 tokens of one index of expert, for one section and micro-batch, no expert is named more than 24 times, a bound that some block reaches.
All inputs are finite; a program needn't handle non-finite values.
Results may differ from a plain program's by a relative error of at most 0.0068.
Values may be sent and summed in bfloat16 or wider, within the bound.
A program may use at most 64 MiB of HBM per device.

v0:
```python
import jax
import jax.numpy as jnp
from jax import lax
from jax.sharding import PartitionSpec as P

EXPERTS = 8
CAP = 24


def shifted_2(value, axis, steps):
    count = lax.axis_size(axis)
    first, last = (max(0, -steps), min(count, count - steps))
    return lax.ppermute(value, axis, [(source, source + steps) for source in range(first, last)])


def slot_index(id_block, experts, capacity):
    flat_ids = id_block.reshape(-1)
    onehot = (flat_ids[:, None] == jnp.arange(experts, dtype=jnp.int32)[None, :]).astype(jnp.int32)
    earlier = jnp.cumsum(onehot, axis=0) - onehot
    within = jnp.sum(earlier * onehot, axis=1)
    return (flat_ids * capacity + within).reshape(id_block.shape)


def route_gates(logits, id_rows):
    chosen = jnp.take_along_axis(logits, id_rows, axis=1)
    row_top = jnp.max(chosen, axis=1, keepdims=True)
    weights = jnp.exp(chosen - row_top)
    return weights / jnp.sum(weights, axis=1, keepdims=True)


def logit_grad(logits, id_rows, gate_vals, prob_grad, z_weight):
    mean_grad = jnp.sum(gate_vals * prob_grad, axis=1, keepdims=True)
    chosen = gate_vals * (prob_grad - mean_grad)
    onehot = (
        id_rows[:, :, None] == jnp.arange(logits.shape[1], dtype=jnp.int32)[None, None, :]
    ).astype(jnp.float32)
    routed = jnp.sum(onehot * chosen[:, :, None], axis=1)
    row_top = jnp.max(logits, axis=1, keepdims=True)
    shifted = jnp.exp(logits - row_top)
    denom_sum = jnp.sum(shifted, axis=1, keepdims=True)
    log_total = row_top + jnp.log(denom_sum)
    return routed + z_weight * 2.0 * log_total * (shifted / denom_sum)


def per_device(
    grad_in,
    head_grad,
    router_logits,
    route_ids,
    gate_act,
    up_act,
    router_weight,
    gate_weight,
    up_weight,
    down_weight,
    z_weight,
):
    members = lax.axis_size("expert")
    slices = members // EXPERTS
    section_idx = lax.axis_index("pipe")
    last_section = lax.axis_size("pipe") - 1
    w_gate = gate_weight[0]
    w_up = up_weight[0]
    w_down = down_weight[0]
    w_router = router_weight[0]
    model_len = w_down.shape[1]

    def local_terms(slot_rows, slot_gate, gate_pre, up_pre):
        raw_grad = jnp.einsum("hd,rd->hr", w_down, slot_rows, preferred_element_type=jnp.float32)
        gate_f = gate_pre.astype(jnp.float32)
        up_f = up_pre.astype(jnp.float32)
        logistic = jax.nn.sigmoid(gate_f)
        swish = gate_f * logistic
        hidden = swish * up_f
        prob_part = jnp.sum(hidden * raw_grad, axis=0).astype(jnp.bfloat16)
        gate_row = slot_gate.astype(jnp.float32)[None, :]
        hid_grad = gate_row * raw_grad
        gate_grad = (hid_grad * up_f * logistic * (1.0 + gate_f * (1.0 - logistic))).astype(
            jnp.bfloat16
        )
        up_grad = (hid_grad * swish).astype(jnp.bfloat16)
        partial_sum = jnp.einsum("hr,hd->rd", gate_grad, w_gate, preferred_element_type=jnp.float32)
        partial_sum = partial_sum + jnp.einsum(
            "hr,hd->rd", up_grad, w_up, preferred_element_type=jnp.float32
        )
        scaled = (hidden * gate_row).astype(jnp.bfloat16)
        return (prob_part, partial_sum.astype(jnp.bfloat16), scaled)

    def micro_step(incoming, micro_idx):
        logits = router_logits[0, micro_idx]
        id_rows = route_ids[0, micro_idx]
        slot_ids = slot_index(id_rows, EXPERTS, CAP)
        gate_vals = route_gates(logits, id_rows)
        sent_gates = gate_vals.astype(jnp.bfloat16)
        onehot = (
            slot_ids[:, :, None] == jnp.arange(EXPERTS * CAP, dtype=jnp.int32)[None, None, :]
        ).astype(jnp.bfloat16)
        row_buffer = jnp.einsum(
            "tks,td->sd", onehot, incoming, preferred_element_type=jnp.float32
        ).astype(jnp.bfloat16)
        gate_buffer = jnp.einsum(
            "tks,tk->s", onehot, sent_gates, preferred_element_type=jnp.float32
        ).astype(jnp.bfloat16)
        send_rows = jnp.repeat(row_buffer.reshape(EXPERTS, CAP, model_len), slices, axis=0)
        send_gates = jnp.repeat(gate_buffer.reshape(EXPERTS, CAP), slices, axis=0)
        got_rows, got_gates = (
            lax.all_to_all(send_rows, "expert", split_axis=0, concat_axis=0, tiled=True),
            lax.all_to_all(send_gates, "expert", split_axis=0, concat_axis=0, tiled=True),
        )
        slot_rows = got_rows.reshape(members * CAP, model_len)
        slot_gate = got_gates.reshape(-1)
        prob_part, partial_sum, scaled = local_terms(
            slot_rows, slot_gate, gate_act[0, micro_idx], up_act[0, micro_idx]
        )
        weight_grad = jnp.einsum("hr,rd->hd", scaled, slot_rows, preferred_element_type=jnp.float32)
        returned, returned_prob = (
            lax.all_to_all(
                partial_sum.reshape(members, CAP, model_len),
                "expert",
                split_axis=0,
                concat_axis=0,
                tiled=True,
            ),
            lax.all_to_all(
                prob_part.reshape(members, CAP), "expert", split_axis=0, concat_axis=0, tiled=True
            ),
        )
        summed = jnp.sum(
            returned.reshape(EXPERTS, slices, CAP, model_len), axis=1, dtype=jnp.float32
        ).reshape(EXPERTS * CAP, model_len)
        summed_prob = jnp.sum(
            returned_prob.reshape(EXPERTS, slices, CAP), axis=1, dtype=jnp.float32
        ).reshape(-1)
        tok_len = incoming.shape[0]
        flat_slots = slot_ids.reshape(-1)
        expert_grad = jnp.sum(
            jnp.take(summed, flat_slots, axis=0).reshape(tok_len, slot_ids.shape[1], model_len),
            axis=1,
        )
        token_prob = jnp.take(summed_prob, flat_slots, axis=0).reshape(slot_ids.shape)
        logit_part = logit_grad(logits, id_rows, gate_vals, token_prob, z_weight).astype(
            jnp.bfloat16
        )
        router_part = jnp.einsum(
            "te,de->td", logit_part, w_router, preferred_element_type=jnp.float32
        )
        input_grad = (incoming.astype(jnp.float32) + expert_grad + router_part).astype(jnp.bfloat16)
        return (input_grad, slot_rows, scaled, weight_grad)

    first_out, rows_first, scaled_first, weight_first = micro_step(grad_in[0], 0)
    handed = shifted_2(first_out, "pipe", -1)
    incoming_second = jnp.where(section_idx == last_section, head_grad, handed)
    second_out, rows_second, scaled_second, weight_second = micro_step(incoming_second, 1)
    weight_total = weight_first + weight_second
    return (second_out[None], weight_total.astype(jnp.bfloat16)[None])


def solution(mesh):
    return jax.shard_map(
        per_device,
        mesh=mesh,
        in_specs=(
            P("pipe", "expert", None),
            P("expert", None),
            P("pipe", None, "expert", None),
            P("pipe", None, "expert", None),
            P("pipe", None, "expert", None),
            P("pipe", None, "expert", None),
            P("pipe", None, None),
            P("pipe", "expert", None),
            P("pipe", "expert", None),
            P("pipe", "expert", None),
            P(),
        ),
        out_specs=(P("pipe", "expert", None), P("pipe", "expert", None)),
        check_vma=False,
    )
```

profile of v0, /device:TPU:0, one launch (start us, length us, event | category | flops | bytes accessed | tf_op | source)
XLA Modules:
  0.0 203.5 jit_solution(10689961889255598056)
XLA Ops:
  0.7 0.8 slice_bitcast_fusion.2
  1.6 0.1 eq.96
  1.9 0.1 eq.86
  2.1 0.2 reduce_window_sum.17
  2.3 0.2 select_reduce_fusion.1
  2.4 0.1 reduce_sum.169
  2.8 0.2 reduce_window_sum.18
  2.9 0.2 select_reduce_fusion
  3.1 0.1 reduce_sum.179
  3.3 0.7 multiply_add_fusion.1
  4.1 2.2 %convolution_convert_fusion.1 = bf16[192,2048]{1,0:T(8,128)(2,1)} fusion(bf16[64,192]{1,0:T(8,128)(2,1)S(1)} %convert_reduce_fusion.1, bf16[1,64,2048]{2,1,0:T(8,128)(2,1)} %param.17), kind=kOutput, calls=%fused_computation.25 | convolution fusion | flops 50331648 | bytes 1073152 | tf_op jit(solution)/shard_map/tks,td->sd/dot_general | solution.py:98
  6.4 7.3 %all-to-all-start.1 = ((bf16[8,24,2048]{2,1,0:T(8,128)(2,1)}), bf16[8,24,2048]{2,1,0:T(8,128)(2,1)}, u32[]{:S(2)}, u32[]{:S(2)}) async-start(bf16[8,24,2048]{2,1,0:T(8,128)(2,1)} %bitcast.222), calls=%async_computation.1 | async-start | bytes 1572864 | tf_op jit(solution)/shard_map/all_to_all | solution.py:107
  13.7 0.1 reshape.355
  13.9 1.0 gather_fusion.3
  14.9 0.1 reshape.358
  15.2 0.2 reshape.346
  15.4 1.0 gather_fusion
  16.4 0.1 reshape.349
  16.7 17.2 %all-to-all-done.1 = bf16[8,24,2048]{2,1,0:T(8,128)(2,1)} async-done(((bf16[8,24,2048]{2,1,0:T(8,128)(2,1)}), bf16[8,24,2048]{2,1,0:T(8,128)(2,1)}, u32[]{:S(2)}, u32[]{:S(2)}) %all-to-all-start.1) | async-done | bytes 786464 | tf_op jit(solution)/shard_map/all_to_all | solution.py:107
  33.9 4.3 %fusion.46 = (bf16[192]{0:T(256)(128)(2,1)S(1)}, f32[768,192]{0,1:T(8,128)}) fusion(bf16[1,2,768,192]{2,3,1,0:T(8,128)(2,1)} %param.22, bf16[1,2,768,192]{2,3,1,0:T(8,128)(2,1)} %param.21, bf16[192,2048]{1,0:T(8,128)(2,1)} %bitcast.7, bf16[1,768,2048]{2,1,0:T(8,128)(2,1)} %param.26), kind=kOutput, calls=%fused_computation.56 | convolution fusion | flops 605306688 | bytes 5112192 | tf_op jit(solution)/shard_map/hd,rd->hr/dot_general | solution.py:69
  38.2 0.7 convert_element_type.246
  38.8 3.6 %all-to-all-start.3 = ((bf16[8,1,24]{2,1,0:T(2,128)(2,1)}), bf16[8,1,24]{2,1,0:T(2,128)(2,1)S(1)}, u32[]{:S(2)}, u32[]{:S(2)}) async-start(bf16[8,1,24]{2,1,0:T(2,128)(2,1)} %convert_element_type.246), calls=%async_computation.3 | async-start | bytes 8192 | tf_op jit(solution)/shard_map/all_to_all | solution.py:124
  42.4 6.4 %all-to-all-done.3 = bf16[8,1,24]{2,1,0:T(2,128)(2,1)S(1)} async-done(((bf16[8,1,24]{2,1,0:T(2,128)(2,1)}), bf16[8,1,24]{2,1,0:T(2,128)(2,1)S(1)}, u32[]{:S(2)}, u32[]{:S(2)}) %all-to-all-start.3) | async-done | bytes 416 | tf_op jit(solution)/shard_map/all_to_all | solution.py:124
  48.9 1.3 gather_fusion.2
  50.2 0.1 reshape.263
  50.4 0.2 fusion.102
  50.7 8.8 %all_to_all.52 = bf16[8,1,24]{2,1,0:T(2,128)(2,1)S(1)} all-to-all(bf16[8,1,24]{2,1,0:T(2,128)(2,1)S(1)} %all_to_all.42), channel_id=1, replica_groups=mesh['pipe'=4,'expert'=8] {'expert'}, dimensions={0} | all-to-all | bytes 768 | tf_op jit(solution)/shard_map/all_to_all | solution.py:108
  59.7 2.2 %fusion.2 = f32[192,2048]{1,0:T(8,128)S(1)} fusion(bf16[1,768,2048]{2,1,0:T(8,128)(2,1)S(1)} %copy-done, f32[768,192]{0,1:T(8,128)} %get-tuple-element.38, f32[192]{0:T(256)S(1)} %reshape.273, bf16[1,2,768,192]{2,3,1,0:T(8,128)(2,1)} %param.21), kind=kOutput, calls=%fused_computation.9 | convolution fusion | flops 605159424 | bytes 5604096 | tf_op jit(solution)/shard_map/hr,hd->rd/dot_general | solution.py:83
  62.0 0.3 copy-done.13
  62.3 1.9 fusion.22
  64.2 4.2 %all-to-all-start.2 = ((bf16[8,24,2048]{2,1,0:T(8,128)(2,1)}), bf16[8,24,2048]{2,1,0:T(8,128)(2,1)}, u32[]{:S(2)}, u32[]{:S(2)}) async-start(bf16[8,24,2048]{2,1,0:T(8,128)(2,1)} %bitcast.225), calls=%async_computation.2 | async-start | bytes 1572864 | tf_op jit(solution)/shard_map/all_to_all | solution.py:117
  69.1 17.4 %all-to-all-done.2 = bf16[8,24,2048]{2,1,0:T(8,128)(2,1)} async-done(((bf16[8,24,2048]{2,1,0:T(8,128)(2,1)}), bf16[8,24,2048]{2,1,0:T(8,128)(2,1)}, u32[]{:S(2)}, u32[]{:S(2)}) %all-to-all-start.2) | async-done | bytes 786464 | tf_op jit(solution)/shard_map/all_to_all | solution.py:117
  86.6 2.5 %bitcast_convert_fusion.1 = f32[192,2048]{1,0:T(8,128)} fusion(bf16[8,24,2048]{2,1,0:T(8,128)(2,1)} %all-to-all-done.2), kind=kLoop, calls=%fused_computation.43 | loop fusion | flops 393216 | bytes 2359296 | tf_op jit(solution)/shard_map/reshape | solution.py:130
  89.0 3.8 %gather_fusion.1 = f32[128,2048]{1,0:T(8,128)} fusion(f32[192,2048]{1,0:T(8,128)} %bitcast_convert_fusion.1, s32[1024]{0:T(1024)S(1)} %pad_clamp_fusion.1), kind=kCustom, calls=%fused_computation.1.clone | custom fusion | bytes 2097664 | tf_op jit(solution)/shard_map/jit(_take)/gather | solution.py:137
  92.8 2.4 %broadcast_select_fusion.1 = f32[128,2048]{1,0:T(8,128)} fusion(f32[128,2048]{1,0:T(8,128)} %gather_fusion.1, pred[128]{0:T(512)(128)(4,1)S(1)} %get-tuple-element.17), kind=kLoop, calls=%fused_computation.83 | loop fusion | flops 262144 | bytes 2097280 | tf_op jit(solution)/shard_map/jit(_take)/select_n | solution.py:137
  95.2 2.8 %reshape.260 = f32[64,2,2048]{2,1,0:T(2,128)} reshape(f32[128,2048]{1,0:T(8,128)} %broadcast_select_fusion.1) | data formatting | bytes 2097152 | tf_op jit(solution)/shard_map/reshape | solution.py:137
  98.0 3.3 %reduce_sum.172 = f32[64,2048]{1,0:T(8,128)} reduce(f32[64,2,2048]{2,1,0:T(2,128)} %reshape.260, f32[]{:T(128)} %constant.39.clone.1), dimensions={1}, to_apply=%region_5.8 | reduce | flops 131072 | bytes 1572868 | tf_op jit(solution)/shard_map/reduce_sum | solution.py:136
  101.3 2.0 fusion.25
  103.3 1.3 collective-permute-start
  104.7 2.2 %collective-permute-done = bf16[64,2048]{1,0:T(8,128)(2,1)S(1)} collective-permute-done((bf16[64,2048]{1,0:T(8,128)(2,1)}, bf16[64,2048]{1,0:T(8,128)(2,1)S(1)}, u32[]{:S(2)}, u32[]{:S(2)}) %collective-permute-start) | collective-permute-done | bytes 262176 | tf_op jit(solution)/shard_map/ppermute | solution.py:13
  107.0 1.3 convolution_convert_fusion
  108.2 4.2 %all-to-all-start.5 = ((bf16[8,24,2048]{2,1,0:T(8,128)(2,1)}), bf16[8,24,2048]{2,1,0:T(8,128)(2,1)}, u32[]{:S(2)}, u32[]{:S(2)}) async-start(bf16[8,24,2048]{2,1,0:T(8,128)(2,1)} %bitcast.223), calls=%async_computation.5 | async-start | bytes 1572864 | tf_op jit(solution)/shard_map/all_to_all | solution.py:107
  112.5 19.5 %all-to-all-done.5 = bf16[8,24,2048]{2,1,0:T(8,128)(2,1)} async-done(((bf16[8,24,2048]{2,1,0:T(8,128)(2,1)}), bf16[8,24,2048]{2,1,0:T(8,128)(2,1)}, u32[]{:S(2)}, u32[]{:S(2)}) %all-to-all-start.5) | async-done | bytes 786464 | tf_op jit(solution)/shard_map/all_to_all | solution.py:107
  132.0 4.3 %fusion.53 = (bf16[192]{0:T(256)(128)(2,1)S(1)}, f32[768,192]{0,1:T(8,128)}) fusion(bf16[1,2,768,192]{2,3,1,0:T(8,128)(2,1)} %param.22, bf16[1,2,768,192]{2,3,1,0:T(8,128)(2,1)} %param.21, bf16[192,2048]{1,0:T(8,128)(2,1)} %bitcast.25, bf16[1,768,2048]{2,1,0:T(8,128)(2,1)} %param.26), kind=kOutput, calls=%fused_computation.63 | convolution fusion | flops 605306688 | bytes 5112192 | tf_op jit(solution)/shard_map/hd,rd->hr/dot_general | solution.py:69
  136.2 0.7 convert_element_type.247
  136.9 4.5 %all-to-all-start.7 = ((bf16[8,1,24]{2,1,0:T(2,128)(2,1)}), bf16[8,1,24]{2,1,0:T(2,128)(2,1)S(1)}, u32[]{:S(2)}, u32[]{:S(2)}) async-start(bf16[8,1,24]{2,1,0:T(2,128)(2,1)} %convert_element_type.247), calls=%async_computation.7 | async-start | bytes 8192 | tf_op jit(solution)/shard_map/all_to_all | solution.py:124
  141.4 6.5 %all-to-all-done.7 = bf16[8,1,24]{2,1,0:T(2,128)(2,1)S(1)} async-done(((bf16[8,1,24]{2,1,0:T(2,128)(2,1)}), bf16[8,1,24]{2,1,0:T(2,128)(2,1)S(1)}, u32[]{:S(2)}, u32[]{:S(2)}) %all-to-all-start.7) | async-done | bytes 416 | tf_op jit(solution)/shard_map/all_to_all | solution.py:124
  148.0 1.3 gather_fusion.5
  149.3 0.1 reshape.271
  149.5 0.2 fusion.100
  149.9 8.8 %all_to_all.53 = bf16[8,1,24]{2,1,0:T(2,128)(2,1)S(1)} all-to-all(bf16[8,1,24]{2,1,0:T(2,128)(2,1)S(1)} %all_to_all.43), channel_id=1, replica_groups=mesh['pipe'=4,'expert'=8] {'expert'}, dimensions={0} | all-to-all | bytes 768 | tf_op jit(solution)/shard_map/all_to_all | solution.py:108
  158.8 2.2 %fusion = f32[192,2048]{1,0:T(8,128)S(1)} fusion(bf16[1,768,2048]{2,1,0:T(8,128)(2,1)S(1)} %copy-done, f32[768,192]{0,1:T(8,128)} %get-tuple-element.40, f32[192]{0:T(256)S(1)} %reshape.280, bf16[1,2,768,192]{2,3,1,0:T(8,128)(2,1)} %param.21), kind=kOutput, calls=%fused_computation.7 | convolution fusion | flops 605159424 | bytes 5604096 | tf_op jit(solution)/shard_map/hr,hd->rd/dot_general | solution.py:83
  161.0 0.3 copy-done.14
  161.4 1.9 fusion.19
  163.3 4.2 %all-to-all-start.6 = ((bf16[8,24,2048]{2,1,0:T(8,128)(2,1)}), bf16[8,24,2048]{2,1,0:T(8,128)(2,1)}, u32[]{:S(2)}, u32[]{:S(2)}) async-start(bf16[8,24,2048]{2,1,0:T(8,128)(2,1)} %bitcast.224), calls=%async_computation.6 | async-start | bytes 1572864 | tf_op jit(solution)/shard_map/all_to_all | solution.py:117
  167.6 2.5 %fusion.73 = f32[768,2048]{1,0:T(8,128)S(1)} fusion(bf16[192,2048]{1,0:T(8,128)(2,1)} %bitcast.7, f32[192]{0:T(256)S(1)} %reshape.273, bf16[1,2,768,192]{2,3,1,0:T(8,128)(2,1)} %param.22, bf16[1,2,768,192]{2,3,1,0:T(8,128)(2,1)} %param.21), kind=kOutput, calls=%fused_computation.86 | convolution fusion | flops 605306880 | bytes 7668480 | tf_op jit(solution)/shard_map/hr,rd->hd/dot_general | solution.py:115
  170.1 3.9 %fusion.12 = bf16[1,768,2048]{2,1,0:T(8,128)(2,1)} fusion(f32[768,2048]{1,0:T(8,128)S(1)} %fusion.73, bf16[192,2048]{1,0:T(8,128)(2,1)} %bitcast.25, f32[192]{0:T(256)S(1)} %reshape.280, bf16[1,2,768,192]{2,3,1,0:T(8,128)(2,1)S(1)} %copy-done.6, bf16[1,2,768,192]{2,3,1,0:T(8,128)(2,1)S(1)} %copy-done.9), kind=kOutput, calls=%fused_computation.19 | convolution fusion | flops 608452608 | bytes 10814464 | tf_op jit(solution)/shard_map/hr,rd->hd/dot_general | solution.py:115
  174.1 12.6 %all-to-all-done.6 = bf16[8,24,2048]{2,1,0:T(8,128)(2,1)} async-done(((bf16[8,24,2048]{2,1,0:T(8,128)(2,1)}), bf16[8,24,2048]{2,1,0:T(8,128)(2,1)}, u32[]{:S(2)}, u32[]{:S(2)}) %all-to-all-start.6) | async-done | bytes 786464 | tf_op jit(solution)/shard_map/all_to_all | solution.py:117
  186.6 2.5 %bitcast_convert_fusion = f32[192,2048]{1,0:T(8,128)} fusion(bf16[8,24,2048]{2,1,0:T(8,128)(2,1)} %all-to-all-done.6), kind=kLoop, calls=%fused_computation.42 | loop fusion | flops 393216 | bytes 2359296 | tf_op jit(solution)/shard_map/reshape | solution.py:130
  189.1 3.8 %gather_fusion.4 = f32[128,2048]{1,0:T(8,128)} fusion(f32[192,2048]{1,0:T(8,128)} %bitcast_convert_fusion, s32[1024]{0:T(1024)S(1)} %pad_clamp_fusion), kind=kCustom, calls=%fused_computation.4.clone | custom fusion | bytes 2097664 | tf_op jit(solution)/shard_map/jit(_take)/gather | solution.py:137
  192.9 2.4 %broadcast_select_fusion = f32[128,2048]{1,0:T(8,128)} fusion(f32[128,2048]{1,0:T(8,128)} %gather_fusion.4, pred[128]{0:T(512)(128)(4,1)S(1)} %get-tuple-element.11), kind=kLoop, calls=%fused_computation.82 | loop fusion | flops 262144 | bytes 2097280 | tf_op jit(solution)/shard_map/jit(_take)/select_n | solution.py:137
  195.2 2.8 %reshape.268 = f32[64,2,2048]{2,1,0:T(2,128)} reshape(f32[128,2048]{1,0:T(8,128)} %broadcast_select_fusion) | data formatting | bytes 2097152 | tf_op jit(solution)/shard_map/reshape | solution.py:137
  198.1 3.3 %reduce_sum.182 = f32[64,2048]{1,0:T(8,128)} reduce(f32[64,2,2048]{2,1,0:T(2,128)} %reshape.268, f32[]{:T(128)} %constant.39.clone.1), dimensions={1}, to_apply=%region_16.20 | reduce | flops 131072 | bytes 1572868 | tf_op jit(solution)/shard_map/reduce_sum | solution.py:136
  201.4 2.1 %fusion.85 = bf16[1,64,2048]{2,1,0:T(8,128)(2,1)} fusion(f32[64,2048]{1,0:T(8,128)} %reduce_sum.182, bf16[64,2048]{1,0:T(8,128)(2,1)S(1)} %copy-done.2, bf16[64,2048]{1,0:T(8,128)(2,1)} %copy-done.3, pred[]{:T(512)S(6)} %eq.42, bf16[1,2048,8]{1,2,0:T(8,128)(2,1)S(1)} %copy-done.10, f32[64,8]{0,1:T(8,128)S(1)} %select_reduce_fusion.2, ...), kind=kOutput, calls=%fused_computation.96 | convolution fusion | flops 2755072 | bytes 1353217 | tf_op jit(solution)/shard_map/te,de->td/dot_general | solution.py:144
  (77 shorter events, 2.3 us)
Async XLA Ops:
  0.6 59.0 %copy-start = (bf16[1,768,2048]{2,1,0:T(8,128)(2,1)S(1)}, bf16[1,768,2048]{2,1,0:T(8,128)(2,1)}, u32[]{:S(2)}) copy-start(bf16[1,768,2048]{2,1,0:T(8,128)(2,1)} %param.25) | copy-start | bytes 9437188
  0.6 13.0 %copy-start.12 = (s32[1,2,64,2]{2,3,1,0:T(2,128)S(1)}, s32[1,2,64,2]{2,3,1,0:T(2,128)}, u32[]{:S(2)}) copy-start(s32[1,2,64,2]{2,3,1,0:T(2,128)} %param.20) | copy-start | bytes 3076
  0.7 13.2 %copy-start.11 = (f32[1,2,64,8]{2,3,1,0:T(8,128)S(1)}, f32[1,2,64,8]{2,3,1,0:T(8,128)}, u32[]{:S(2)}) copy-start(f32[1,2,64,8]{2,3,1,0:T(8,128)} %param.19) | copy-start | bytes 12292
  6.4 27.5 %all-to-all-start.1 = ((bf16[8,24,2048]{2,1,0:T(8,128)(2,1)}), bf16[8,24,2048]{2,1,0:T(8,128)(2,1)}, u32[]{:S(2)}, u32[]{:S(2)}) async-start(bf16[8,24,2048]{2,1,0:T(8,128)(2,1)} %bitcast.222), calls=%async_computation.1 | async-start | bytes 1572864 | tf_op jit(solution)/shard_map/all_to_all | solution.py:107
  38.8 9.9 %all-to-all-start.3 = ((bf16[8,1,24]{2,1,0:T(2,128)(2,1)}), bf16[8,1,24]{2,1,0:T(2,128)(2,1)S(1)}, u32[]{:S(2)}, u32[]{:S(2)}) async-start(bf16[8,1,24]{2,1,0:T(2,128)(2,1)} %convert_element_type.246), calls=%async_computation.3 | async-start | bytes 8192 | tf_op jit(solution)/shard_map/all_to_all | solution.py:124
  59.7 2.3 %copy-start.4 = (bf16[1,2,768,192]{2,3,1,0:T(8,128)(2,1)S(1)}, bf16[1,2,768,192]{2,3,1,0:T(8,128)(2,1)}, u32[]{:S(2)}) copy-start(bf16[1,2,768,192]{2,3,1,0:T(8,128)(2,1)} %param.22) | copy-start | bytes 1769476
  59.7 2.3 %copy-start.7 = (bf16[1,2,768,192]{2,3,1,0:T(8,128)(2,1)S(1)}, bf16[1,2,768,192]{2,3,1,0:T(8,128)(2,1)}, u32[]{:S(2)}) copy-start(bf16[1,2,768,192]{2,3,1,0:T(8,128)(2,1)} %param.21) | copy-start | bytes 1769476
  59.7 2.5 %copy-start.13 = (bf16[1,768,2048]{2,1,0:T(8,128)(2,1)S(1)}, bf16[1,768,2048]{2,1,0:T(8,128)(2,1)}, u32[]{:S(2)}) copy-start(bf16[1,768,2048]{2,1,0:T(8,128)(2,1)} %param.24) | copy-start | bytes 9437188
  59.7 2.6 %copy-start.15 = (f32[768,192]{0,1:T(8,128)S(1)}, f32[768,192]{0,1:T(8,128)}, u32[]{:S(2)}) copy-start(f32[768,192]{0,1:T(8,128)} %get-tuple-element.38) | copy-start | bytes 1769476
  64.2 22.3 %all-to-all-start.2 = ((bf16[8,24,2048]{2,1,0:T(8,128)(2,1)}), bf16[8,24,2048]{2,1,0:T(8,128)(2,1)}, u32[]{:S(2)}, u32[]{:S(2)}) async-start(bf16[8,24,2048]{2,1,0:T(8,128)(2,1)} %bitcast.225), calls=%async_computation.2 | async-start | bytes 1572864 | tf_op jit(solution)/shard_map/all_to_all | solution.py:117
  92.8 8.5 %copy-start.1 = (bf16[1,64,2048]{2,1,0:T(8,128)(2,1)S(1)}, bf16[1,64,2048]{2,1,0:T(8,128)(2,1)}, u32[]{:S(2)}) copy-start(bf16[1,64,2048]{2,1,0:T(8,128)(2,1)} %param.17) | copy-start | bytes 786436
  92.8 8.5 %copy-start.10 = (bf16[1,2048,8]{1,2,0:T(8,128)(2,1)S(1)}, bf16[1,2048,8]{1,2,0:T(8,128)(2,1)}, u32[]{:S(2)}) copy-start(bf16[1,2048,8]{1,2,0:T(8,128)(2,1)} %param.23) | copy-start | bytes 98308
  103.3 3.6 %collective-permute-start = (bf16[64,2048]{1,0:T(8,128)(2,1)}, bf16[64,2048]{1,0:T(8,128)(2,1)S(1)}, u32[]{:S(2)}, u32[]{:S(2)}) collective-permute-start(bf16[64,2048]{1,0:T(8,128)(2,1)} %fusion.25), channel_id=1, source_target_pairs={{8,0},{16,8},{24,16},{9,1},{17,9},{25,17},{10,2},{18,10},{26,18},{... | collective-permute-start | bytes 786440 | tf_op jit(solution)/shard_map/ppermute | solution.py:13
  107.0 29.2 %copy-start.3 = (bf16[64,2048]{1,0:T(8,128)(2,1)}, bf16[64,2048]{1,0:T(8,128)(2,1)S(1)}, u32[]{:S(2)}) copy-start(bf16[64,2048]{1,0:T(8,128)(2,1)S(1)} %collective-permute-done) | copy-start | bytes 786436
  108.2 23.7 %all-to-all-start.5 = ((bf16[8,24,2048]{2,1,0:T(8,128)(2,1)}), bf16[8,24,2048]{2,1,0:T(8,128)(2,1)}, u32[]{:S(2)}, u32[]{:S(2)}) async-start(bf16[8,24,2048]{2,1,0:T(8,128)(2,1)} %bitcast.223), calls=%async_computation.5 | async-start | bytes 1572864 | tf_op jit(solution)/shard_map/all_to_all | solution.py:107
  136.9 11.0 %all-to-all-start.7 = ((bf16[8,1,24]{2,1,0:T(2,128)(2,1)}), bf16[8,1,24]{2,1,0:T(2,128)(2,1)S(1)}, u32[]{:S(2)}, u32[]{:S(2)}) async-start(bf16[8,1,24]{2,1,0:T(2,128)(2,1)} %convert_element_type.247), calls=%async_computation.7 | async-start | bytes 8192 | tf_op jit(solution)/shard_map/all_to_all | solution.py:124
  158.8 2.2 %copy-start.5 = (bf16[1,2,768,192]{2,3,1,0:T(8,128)(2,1)S(1)}, bf16[1,2,768,192]{2,3,1,0:T(8,128)(2,1)}, u32[]{:S(2)}) copy-start(bf16[1,2,768,192]{2,3,1,0:T(8,128)(2,1)} %param.22) | copy-start | bytes 1769476
  158.8 2.3 %copy-start.8 = (bf16[1,2,768,192]{2,3,1,0:T(8,128)(2,1)S(1)}, bf16[1,2,768,192]{2,3,1,0:T(8,128)(2,1)}, u32[]{:S(2)}) copy-start(bf16[1,2,768,192]{2,3,1,0:T(8,128)(2,1)} %param.21) | copy-start | bytes 1769476
  158.8 2.5 %copy-start.14 = (bf16[1,768,2048]{2,1,0:T(8,128)(2,1)S(1)}, bf16[1,768,2048]{2,1,0:T(8,128)(2,1)}, u32[]{:S(2)}) copy-start(bf16[1,768,2048]{2,1,0:T(8,128)(2,1)} %param.24) | copy-start | bytes 9437188
  158.8 2.6 %copy-start.16 = (f32[768,192]{0,1:T(8,128)S(1)}, f32[768,192]{0,1:T(8,128)}, u32[]{:S(2)}) copy-start(f32[768,192]{0,1:T(8,128)} %get-tuple-element.40) | copy-start | bytes 1769476
  163.3 23.3 %all-to-all-start.6 = ((bf16[8,24,2048]{2,1,0:T(8,128)(2,1)}), bf16[8,24,2048]{2,1,0:T(8,128)(2,1)}, u32[]{:S(2)}, u32[]{:S(2)}) async-start(bf16[8,24,2048]{2,1,0:T(8,128)(2,1)} %bitcast.224), calls=%async_computation.6 | async-start | bytes 1572864 | tf_op jit(solution)/shard_map/all_to_all | solution.py:117
  167.6 2.6 %copy-start.6 = (bf16[1,2,768,192]{2,3,1,0:T(8,128)(2,1)S(1)}, bf16[1,2,768,192]{2,3,1,0:T(8,128)(2,1)}, u32[]{:S(2)}) copy-start(bf16[1,2,768,192]{2,3,1,0:T(8,128)(2,1)} %param.22) | copy-start | bytes 1769476
  167.6 2.6 %copy-start.9 = (bf16[1,2,768,192]{2,3,1,0:T(8,128)(2,1)S(1)}, bf16[1,2,768,192]{2,3,1,0:T(8,128)(2,1)}, u32[]{:S(2)}) copy-start(bf16[1,2,768,192]{2,3,1,0:T(8,128)(2,1)} %param.21) | copy-start | bytes 1769476
  192.9 8.5 %copy-start.2 = (bf16[64,2048]{1,0:T(8,128)(2,1)S(1)}, bf16[64,2048]{1,0:T(8,128)(2,1)}, u32[]{:S(2)}) copy-start(bf16[64,2048]{1,0:T(8,128)(2,1)} %param.18) | copy-start | bytes 786436
where the time goes:
time: 205 us; the launch traced here: 203 us
  waiting for transfers between devices  81.8 us (40%)
  matrix products  31.2 us (15%)
  starting transfers between devices  29.2 us (14%)
  local copies, waits for them, and re-layouts  23.5 us (11%)
  other arithmetic  18.4 us (9%)
  blocking collectives  17.7 us (9%)
    all_to_all x2, waiting for transfers between devices, micro_step(): lax.all_to_all(send_rows, 'expert', split_axis=0, concat_axis=0, tiled=True)  36.7 us
    all_to_all x2, waiting for transfers between devices, micro_step(): lax.all_to_all(partial_sum.reshape(members, CAP, model_len), 'expert', sp...  30 us
    all_to_all x2, blocking collectives, micro_step(): lax.all_to_all(send_gates, 'expert', split_axis=0, concat_axis=0, tiled=T...  17.7 us
    all_to_all x2, waiting for transfers between devices, micro_step(): lax.all_to_all(prob_part.reshape(members, CAP), 'expert', split_axis=0, c...  12.8 us
    all_to_all x2, starting transfers between devices, micro_step(): lax.all_to_all(send_rows, 'expert', split_axis=0, concat_axis=0, tiled=True)  11.5 us
    dot_general x2, matrix products, local_terms(): jnp.einsum('hd,rd->hr', w_down, slot_rows, preferred_element_type=jnp.flo...  8.51 us
    all_to_all x2, starting transfers between devices, micro_step(): lax.all_to_all(partial_sum.reshape(members, CAP, model_len), 'expert', sp...  8.4 us
    all_to_all x2, starting transfers between devices, micro_step(): lax.all_to_all(prob_part.reshape(members, CAP), 'expert', split_axis=0, c...  8.1 us
  transfers between devices with their start and end apart: 7, of which 7 were waited for; matrix products, arithmetic and copies ran while one was open for 5% of the time, Pallas kernels for 0%

commit v1 on v0

v1 whole, which is shorter than its diff:
```python
import functools

import jax
import jax.numpy as jnp
from jax import lax
from jax.experimental import pallas as pl
from jax.experimental.pallas import tpu as pltpu
from jax.sharding import PartitionSpec as P

EXPERTS = 8
CAP = 24
TOP = 2
F32 = jnp.float32
BF16 = jnp.bfloat16
D0, R0, D1, R1 = 0, 1, 2, 3


def iota_f(shape, dim):
    return lax.broadcasted_iota(jnp.int32, shape, dim).astype(F32)


def dot(a, b):
    return jnp.dot(a, b, preferred_element_type=F32)


def kernel(
    n, pipes,
    grad_ref, head_ref, logits_ref, ids_ref, zw_ref, wr_ref, ga_hbm, ua_hbm, wg_hbm, wu_hbm, wd_hbm,
    out_ref, dg_hbm,
    sbuf, rbuf, gsend, grecv, psend, precv, hsend, hrecv, g1_ref,
    x_ref, scaled_ref, ggt_ref, ugt_ref, dgv, ga_ref, ua_ref, wg_ref, wu_ref, wd_ref,
    ssem, rsem, gssem, grsem, pssem, prsem, hsem, lsem,
):
    me = lax.axis_index("expert")
    pipe = lax.axis_index("pipe")
    down = lax.rem(pipe + pipes - 1, pipes)
    up = lax.rem(pipe + 1, pipes)
    slices = n // EXPERTS
    tok, dim = grad_ref.shape
    hid = wd_ref.shape[0]
    width = n * CAP
    cols = 512 if dim % 512 == 0 else dim
    ht = 256 if hid % 256 == 0 else hid

    loads = [
        pltpu.make_async_copy(src, dst, lsem.at[i])
        for i, (src, dst) in enumerate(
            [(wd_hbm, wd_ref), (ga_hbm, ga_ref), (ua_hbm, ua_ref), (wg_hbm, wg_ref), (wu_hbm, wu_ref)]
        )
    ]
    for load in loads:
        load.start()

    barrier = pltpu.get_barrier_semaphore()

    def greet(p, carry):
        pl.semaphore_signal(
            barrier, inc=1, device_id=(pipe, lax.rem(me + p, n)), device_id_type=pl.DeviceIdType.MESH
        )
        return carry

    lax.fori_loop(1, n, greet, 0)
    for other in (down, up):
        pl.semaphore_signal(barrier, inc=1, device_id=(other, me), device_id_type=pl.DeviceIdType.MESH)

    def peer_copy(src, dst, s, r, p):
        return pltpu.make_async_remote_copy(
            src_ref=src, dst_ref=dst, send_sem=s, recv_sem=r,
            device_id=(pipe, p), device_id_type=pl.DeviceIdType.MESH,
        )

    def each_peer(body):
        def step(p, carry):
            body(lax.rem(me + p, n))
            return carry

        lax.fori_loop(1, n, step, 0)

    def tiles(total, size, body):
        def step(i, carry):
            body(pl.ds(pl.multiple_of(i * size, size), size))
            return carry

        lax.fori_loop(0, total // size, step, 0)

    def route(m):
        z = logits_ref[m]
        ids = ids_ref[m].astype(F32)
        ecol = iota_f((tok, EXPERTS), 1)
        picks = [ids[:, k : k + 1] for k in range(TOP)]
        named = [jnp.where(i == ecol, 1.0, 0.0) for i in picks]
        lower = jnp.where(iota_f((tok, tok), 0) > iota_f((tok, tok), 1), 1.0, 0.0).astype(BF16)
        earlier = dot(lower, (named[0] + named[1]).astype(BF16))
        ranks = [jnp.sum(a * earlier, axis=1, keepdims=True) for a in named]
        chosen = [jnp.sum(a * z, axis=1, keepdims=True) for a in named]
        top = jnp.maximum(chosen[0], chosen[1])
        w = [jnp.exp(c - top) for c in chosen]
        gates = [v / (w[0] + w[1]) for v in w]
        q = iota_f((tok, EXPERTS * CAP), 1)
        spread = sum(jnp.where(i * CAP + r == q, 1.0, 0.0) for i, r in zip(picks, ranks))
        if slices == 1:
            gather = spread.astype(BF16)
        else:
            q = iota_f((tok, width), 1)
            member = jnp.floor((q + 0.5) / CAP)
            place = jnp.floor((member + 0.5) / slices) * CAP + (q - member * CAP)
            gather = sum(jnp.where(i * CAP + r == place, 1.0, 0.0) for i, r in zip(picks, ranks)).astype(BF16)
        owner = jnp.floor((iota_f((tok, n), 1) + 0.5) / slices)
        owned = [jnp.where(i == owner, 1.0, 0.0) for i in picks]
        lane = iota_f((tok, width), 1)
        base = (me * CAP).astype(F32)
        at = [jnp.where(r + base == lane, 1.0, 0.0) for r in ranks]
        gate_rows = sum(
            dot((o * g.astype(BF16).astype(F32)).T.astype(BF16), a.astype(BF16))
            for o, g, a in zip(owned, gates, at)
        )
        z_top = jnp.max(z, axis=1, keepdims=True)
        shifted = jnp.exp(z - z_top)
        denom = jnp.sum(shifted, axis=1, keepdims=True)
        z_term = zw_ref[0, 0] * 2.0 * (z_top + jnp.log(denom)) * (shifted / denom)
        return dict(
            named=named, gates=gates, spread_t=spread.T.astype(BF16), gather=gather, owned=owned, at=at,
            gate_rows=gate_rows, z_term=z_term,
        )

    def send_rows(phase, by_expert):
        def go(d):
            src = sbuf.at[phase, d // slices if by_expert else d]
            peer_copy(src, rbuf.at[phase, me], ssem.at[phase, d], rsem.at[phase, me], d).start()

        each_peer(go)

    def wait_rows(phase):
        def go(d):
            peer_copy(rbuf.at[phase, d], rbuf.at[phase, d], ssem.at[phase, d], rsem.at[phase, d], d).wait_recv()

        each_peer(go)

    def dispatch(phase, spread_t, src):
        def body(c):
            rows = dot(spread_t, src[:, c])
            for e in range(EXPERTS):
                sbuf[phase, e, :, c] = rows[e * CAP : (e + 1) * CAP].astype(BF16)

        tiles(dim, cols, body)
        send_rows(phase, True)
        rbuf[phase, me] = sbuf[phase, me // slices]

    def joined(phase, c):
        return jnp.concatenate([rbuf[phase, j, :, c].astype(F32) for j in range(n)], axis=0).astype(BF16)

    def local(m, phase, gate_row):
        def fill(c):
            x_ref[m, :, c] = joined(phase, c)

        tiles(dim, cols, fill)
        prob = jnp.zeros((1, width), F32)
        for h in range(0, hid, ht):
            rows = pl.ds(h, ht)
            raw = lax.dot_general(
                wd_ref[rows, :], x_ref[m], (((1,), (1,)), ((), ())), preferred_element_type=F32
            )
            g = ga_ref[m, rows, :].astype(F32)
            u = ua_ref[m, rows, :].astype(F32)
            logistic = jax.nn.sigmoid(g)
            swish = g * logistic
            hidden = swish * u
            prob = prob + jnp.sum(hidden * raw, axis=0, keepdims=True)
            hid_grad = gate_row * raw
            gate_grad = hid_grad * u * logistic * (1.0 + g * (1.0 - logistic))
            up_grad = hid_grad * swish
            scaled_ref[m, rows, :] = (hidden * gate_row).astype(BF16)
            ggt_ref[:, rows] = gate_grad.T.astype(BF16)
            ugt_ref[:, rows] = up_grad.T.astype(BF16)
        psend[m] = jnp.broadcast_to(prob, (16, width)).astype(BF16)

    def give_back(m, phase):
        def go(d):
            peer_copy(psend.at[m], precv.at[m, me], pssem.at[m, d], prsem.at[m, me], d).start()

        each_peer(go)

        def body(c):
            part = dot(ggt_ref[...], wg_ref[:, c]) + dot(ugt_ref[...], wu_ref[:, c])
            for j in range(n):
                sbuf[phase, j, :, c] = part[j * CAP : (j + 1) * CAP].astype(BF16)

        tiles(dim, cols, body)
        send_rows(phase, False)
        rbuf[phase, me] = sbuf[phase, me]
        precv[m, me] = psend[m]

    def combine(m, phase, info, src, dst):
        def arrived(d):
            peer_copy(psend.at[m], precv.at[m, d], pssem.at[m, d], prsem.at[m, d], d).wait_recv()

        each_peer(arrived)
        probs = [jnp.zeros((tok, width), F32) for _ in range(TOP)]
        for d in range(n):
            row = precv[m, d].astype(F32)[0:1]
            probs = [p + o[:, d : d + 1] * row for p, o in zip(probs, info["owned"])]
        probs = [jnp.sum(p * a, axis=1, keepdims=True) for p, a in zip(probs, info["at"])]
        gates = info["gates"]
        mean = gates[0] * probs[0] + gates[1] * probs[1]
        logit = info["z_term"]
        for k in range(TOP):
            logit = logit + info["named"][k] * (gates[k] * (probs[k] - mean))
        logit = logit.astype(BF16)
        wait_rows(phase)

        def body(c):
            total = src[:, c].astype(F32) + dot(info["gather"], joined(phase, c))
            dst[:, c] = (total + dot(logit, wr_ref[:, c])).astype(BF16)

        tiles(dim, cols, body)

    first = route(0)
    pl.semaphore_wait(barrier, n + 1)
    dispatch(D0, first["spread_t"], grad_ref)
    second = route(1)
    half = lax.broadcasted_iota(jnp.int32, (16, width), 0) < 8
    for d in range(n):
        gsend[d] = jnp.where(half, first["gate_rows"][d : d + 1], second["gate_rows"][d : d + 1]).astype(BF16)

    def go_gates(d):
        peer_copy(gsend.at[d], grecv.at[me], gssem.at[d], grsem.at[me], d).start()

    each_peer(go_gates)
    grecv[me] = gsend[me]

    def come_gates(d):
        peer_copy(gsend.at[d], grecv.at[d], gssem.at[d], grsem.at[d], d).wait_recv()

    each_peer(come_gates)
    gate_all = jnp.zeros((16, width), F32)
    for j in range(n):
        gate_all = gate_all + grecv[j].astype(F32)

    for load in loads:
        load.wait()
    wait_rows(D0)
    local(0, D0, gate_all[0:1])
    give_back(0, R0)
    combine(0, R0, first, grad_ref, hsend)
    pass_on = pltpu.make_async_remote_copy(
        src_ref=hsend, dst_ref=hrecv, send_sem=hsem.at[0], recv_sem=hsem.at[1],
        device_id=(down, me), device_id_type=pl.DeviceIdType.MESH,
    )
    pass_on.start()
    pass_on.wait_recv()
    is_last = pipe == pipes - 1
    g1_ref[...] = jnp.where(is_last, head_ref[...], hrecv[...])
    dispatch(D1, second["spread_t"], g1_ref)
    wait_rows(D1)
    local(1, D1, gate_all[8:9])
    give_back(1, R1)

    def weigh(c):
        total = dot(scaled_ref[0], x_ref[0, :, c]) + dot(scaled_ref[1], x_ref[1, :, c])
        dgv[:, c] = total.astype(BF16)

    tiles(dim, 256 if dim % 256 == 0 else dim, weigh)
    store = pltpu.make_async_copy(dgv, dg_hbm, lsem.at[0])
    store.start()
    combine(1, R1, second, g1_ref, out_ref)
    store.wait()
    pass_on.wait_send()

    def drain(d):
        for phase in range(4):
            src = sbuf.at[phase, d]
            peer_copy(src, src, ssem.at[phase, d], rsem.at[phase, d], d).wait_send()
        for m in range(2):
            peer_copy(psend.at[m], precv.at[m, d], pssem.at[m, d], prsem.at[m, d], d).wait_send()
        peer_copy(gsend.at[d], grecv.at[d], gssem.at[d], grsem.at[d], d).wait_send()

    each_peer(drain)


def per_device(
    grad_in, head_grad, router_logits, route_ids, gate_act, up_act, router_weight,
    gate_weight, up_weight, down_weight, z_weight,
):
    n = lax.axis_size("expert")
    pipes = lax.axis_size("pipe")
    tok, dim = head_grad.shape
    hid = down_weight.shape[1]
    width = n * CAP
    vmem = pl.BlockSpec(memory_space=pltpu.VMEM)
    smem = pl.BlockSpec(memory_space=pltpu.SMEM)
    hbm = pl.BlockSpec(memory_space=pl.ANY)
    dma = pltpu.SemaphoreType.DMA
    out, dg = pl.pallas_call(
        functools.partial(kernel, n, pipes),
        out_shape=(
            jax.ShapeDtypeStruct((tok, dim), BF16),
            jax.ShapeDtypeStruct((hid, dim), BF16),
        ),
        in_specs=[vmem, vmem, vmem, vmem, smem, vmem, hbm, hbm, hbm, hbm, hbm],
        out_specs=(vmem, hbm),
        scratch_shapes=[
            pltpu.VMEM((4, n, CAP, dim), BF16),
            pltpu.VMEM((4, n, CAP, dim), BF16),
            pltpu.VMEM((n, 16, width), BF16),
            pltpu.VMEM((n, 16, width), BF16),
            pltpu.VMEM((2, 16, width), BF16),
            pltpu.VMEM((2, n, 16, width), BF16),
            pltpu.VMEM((tok, dim), BF16),
            pltpu.VMEM((tok, dim), BF16),
            pltpu.VMEM((tok, dim), BF16),
            pltpu.VMEM((2, width, dim), BF16),
            pltpu.VMEM((2, hid, width), BF16),
            pltpu.VMEM((width, hid), BF16),
            pltpu.VMEM((width, hid), BF16),
            pltpu.VMEM((hid, dim), BF16),
            pltpu.VMEM((2, hid, width), BF16),
            pltpu.VMEM((2, hid, width), BF16),
            pltpu.VMEM((hid, dim), BF16),
            pltpu.VMEM((hid, dim), BF16),
            pltpu.VMEM((hid, dim), BF16),
            dma((4, n)), dma((4, n)), dma((n,)), dma((n,)), dma((2, n)), dma((2, n)), dma((2,)), dma((5,)),
        ],
        compiler_params=pltpu.CompilerParams(
            collective_id=0, has_side_effects=True, vmem_limit_bytes=56 * 1024 * 1024
        ),
        cost_estimate=pl.CostEstimate(
            flops=16 * hid * width * dim, bytes_accessed=8 * hid * dim, transcendentals=2 * hid * width
        ),
    )(
        grad_in[0], head_grad, router_logits[0], route_ids[0], z_weight.reshape(1, 1),
        router_weight[0].T, gate_act[0], up_act[0], gate_weight[0], up_weight[0], down_weight[0],
    )
    return out[None], dg[None]


def solution(mesh):
    return jax.shard_map(
        per_device,
        mesh=mesh,
        in_specs=(
            P("pipe", "expert", None),
            P("expert", None),
            P("pipe", None, "expert", None),
            P("pipe", None, "expert", None),
            P("pipe", None, "expert", None),
            P("pipe", None, "expert", None),
            P("pipe", None, None),
            P("pipe", "expert", None),
            P("pipe", "expert", None),
            P("pipe", "expert", None),
            P(),
        ),
        out_specs=(P("pipe", "expert", None), P("pipe", "expert", None)),
        check_vma=False,
    )
```

time: 205 us -> 108 us (0.53)
  the two profiles are of different devices: /device:TPU:0 before, /device:TPU:19 now
where the time goes in v1:
time: 108 us; the launch traced here: 107 us
  Pallas kernels  93.2 us (86%)
  local copies, waits for them, and re-layouts  12.9 us (12%)
  between operations  1.29 us (1%)
    pallas_call x1, Pallas kernels, per_device(): pl.pallas_call(functools.partial(kernel, n, pipes), out_shape=(jax.ShapeD...  93.2 us
    unnamed x6, local copies, waits for them, and re-layouts  12.9 us

profile of v1, /device:TPU:19, one launch (start us, length us, event | category | flops | bytes accessed | tf_op | source)
XLA Modules:
  0.0 107.4 jit_solution(14551931809226513235)
XLA Ops:
  1.3 1.4 %copy.13 = f32[1,2,64,8]{3,2,1,0:T(8,128)} copy(f32[1,2,64,8]{2,3,1,0:T(8,128)} %param.13) | data formatting | bytes 8192 | tf_op args[2]
  2.7 1.4 %copy.14 = s32[1,2,64,2]{3,2,1,0:T(8,128)} copy(s32[1,2,64,2]{2,3,1,0:T(2,128)} %param.14) | data formatting | bytes 2048 | tf_op args[3]
  4.1 2.2 %copy.15 = bf16[1,2,768,192]{3,2,1,0:T(8,128)(2,1)} copy(bf16[1,2,768,192]{2,3,1,0:T(8,128)(2,1)} %param.15) | data formatting | bytes 1179648 | tf_op args[4]
  6.3 2.2 %copy.16 = bf16[1,2,768,192]{3,2,1,0:T(8,128)(2,1)} copy(bf16[1,2,768,192]{2,3,1,0:T(8,128)(2,1)} %param.16) | data formatting | bytes 1179648 | tf_op args[5]
  8.6 93.2 %shard_map.122 = (bf16[64,2048]{1,0:T(8,128)(2,1)}, bf16[768,2048]{1,0:T(8,128)(2,1)}) custom-call(bf16[64,2048]{1,0:T(8,128)(2,1)} %bitcast.24, bf16[64,2048]{1,0:T(8,128)(2,1)} %head_ref.1, f32[2,64,8]{2,1,0:T(8,128)} %bitcast.19, s32[2,64,2]{2,1,0:T(8,128)} %bitcast.20, f32[1,1]{1,0:T(1,128)} %bitcast.14.zw_ref, bf16[8,2048]{1,0:T(8,128)(2,1)} %bitcast.25, ...), custom_call_target="tpu_custom_call" | custom-call | flops 4831838208 | bytes 12582912 | tf_op jit(solution)/shard_map/pallas_call | solution.py:293
  101.8 1.7 %copy.20 = bf16[1,64,2048]{2,1,0:T(8,128)(2,1)} copy(bf16[1,64,2048]{2,1,0:T(8,128)(2,1)} %bitcast.18) | data formatting | bytes 524288
  103.5 4.0 %copy.21 = bf16[1,768,2048]{2,1,0:T(8,128)(2,1)} copy(bf16[1,768,2048]{2,1,0:T(8,128)(2,1)} %bitcast.15) | data formatting | bytes 6291456

commit v2 on v1

--- a/solution.py
+++ b/solution.py
@@ -13,6 +13,7 @@
 F32 = jnp.float32
 BF16 = jnp.bfloat16
 D0, R0, D1, R1 = 0, 1, 2, 3
+HALVES = 2
 
 
 def iota_f(shape, dim):
@@ -28,7 +29,7 @@
     grad_ref, head_ref, logits_ref, ids_ref, zw_ref, wr_ref, ga_hbm, ua_hbm, wg_hbm, wu_hbm, wd_hbm,
     out_ref, dg_hbm,
     sbuf, rbuf, gsend, grecv, psend, precv, hsend, hrecv, g1_ref,
-    x_ref, scaled_ref, ggt_ref, ugt_ref, dgv, ga_ref, ua_ref, wg_ref, wu_ref, wd_ref,
+    x_ref, scaled_ref, st_ref, ggt_ref, ugt_ref, dgv, ga_ref, ua_ref, wg_ref, wu_ref, wd_ref,
     ssem, rsem, gssem, grsem, pssem, prsem, hsem, lsem,
 ):
     me = lax.axis_index("expert")
@@ -39,7 +40,8 @@
     tok, dim = grad_ref.shape
     hid = wd_ref.shape[0]
     width = n * CAP
-    cols = 512 if dim % 512 == 0 else dim
+    part = dim // HALVES
+    cols = 512 if part % 512 == 0 else part
     ht = 256 if hid % 256 == 0 else hid
 
     loads = [
@@ -84,10 +86,10 @@
         lax.fori_loop(0, total // size, step, 0)
 
     def route(m):
-        z = logits_ref[m]
+        z = logits_ref[m].T
         ids = ids_ref[m].astype(F32)
         ecol = iota_f((tok, EXPERTS), 1)
-        picks = [ids[:, k : k + 1] for k in range(TOP)]
+        picks = [jnp.broadcast_to(ids[k : k + 1], (EXPERTS, tok)).T[:, 0:1] for k in range(TOP)]
         named = [jnp.where(i == ecol, 1.0, 0.0) for i in picks]
         lower = jnp.where(iota_f((tok, tok), 0) > iota_f((tok, tok), 1), 1.0, 0.0).astype(BF16)
         earlier = dot(lower, (named[0] + named[1]).astype(BF16))
@@ -123,74 +125,83 @@
             gate_rows=gate_rows, z_term=z_term,
         )
 
-    def send_rows(phase, by_expert):
+    def send_rows(phase, h, by_expert):
         def go(d):
-            src = sbuf.at[phase, d // slices if by_expert else d]
-            peer_copy(src, rbuf.at[phase, me], ssem.at[phase, d], rsem.at[phase, me], d).start()
+            src = sbuf.at[phase, h, d // slices if by_expert else d]
+            peer_copy(src, rbuf.at[phase, h, me], ssem.at[phase, h, d], rsem.at[phase, h, me], d).start()
 
         each_peer(go)
 
-    def wait_rows(phase):
+    def wait_rows(phase, h):
         def go(d):
-            peer_copy(rbuf.at[phase, d], rbuf.at[phase, d], ssem.at[phase, d], rsem.at[phase, d], d).wait_recv()
+            ref = rbuf.at[phase, h, d]
+            peer_copy(ref, ref, ssem.at[phase, h, d], rsem.at[phase, h, d], d).wait_recv()
 
         each_peer(go)
 
-    def dispatch(phase, spread_t, src):
+    def half_tiles(body):
+        for i in range(part // cols):
+            body(slice(i * cols, (i + 1) * cols))
+
+    def dispatch(phase, h, spread_t, src):
         def body(c):
-            rows = dot(spread_t, src[:, c])
+            rows = dot(spread_t, src[:, h * part + c.start : h * part + c.stop])
             for e in range(EXPERTS):
-                sbuf[phase, e, :, c] = rows[e * CAP : (e + 1) * CAP].astype(BF16)
-
-        tiles(dim, cols, body)
-        send_rows(phase, True)
-        rbuf[phase, me] = sbuf[phase, me // slices]
-
-    def joined(phase, c):
-        return jnp.concatenate([rbuf[phase, j, :, c].astype(F32) for j in range(n)], axis=0).astype(BF16)
-
-    def local(m, phase, gate_row):
-        def fill(c):
-            x_ref[m, :, c] = joined(phase, c)
-
-        tiles(dim, cols, fill)
-        prob = jnp.zeros((1, width), F32)
+                sbuf[phase, h, e, :, c] = rows[e * CAP : (e + 1) * CAP].astype(BF16)
+
+        half_tiles(body)
+        send_rows(phase, h, True)
+        rbuf[phase, h, me] = sbuf[phase, h, me // slices]
+
+    def joined(phase, h, c):
+        return jnp.concatenate([rbuf[phase, h, j, :, c].astype(F32) for j in range(n)], axis=0).astype(BF16)
+
+    def local(m, phase, gate_col):
+        for h in range(HALVES):
+            wait_rows(phase, h)
+
+            def fill(c):
+                x_ref[m, :, h * part + c.start : h * part + c.stop] = joined(phase, h, c)
+
+            half_tiles(fill)
+        prob = jnp.zeros((width, 1), F32)
         for h in range(0, hid, ht):
-            rows = pl.ds(h, ht)
+            rows = slice(h, h + ht)
             raw = lax.dot_general(
-                wd_ref[rows, :], x_ref[m], (((1,), (1,)), ((), ())), preferred_element_type=F32
+                x_ref[m], wd_ref[rows, :], (((1,), (1,)), ((), ())), preferred_element_type=F32
             )
-            g = ga_ref[m, rows, :].astype(F32)
-            u = ua_ref[m, rows, :].astype(F32)
+            g = ga_ref[m, :, rows].astype(F32)
+            u = ua_ref[m, :, rows].astype(F32)
             logistic = jax.nn.sigmoid(g)
             swish = g * logistic
             hidden = swish * u
-            prob = prob + jnp.sum(hidden * raw, axis=0, keepdims=True)
-            hid_grad = gate_row * raw
+            prob = prob + jnp.sum(hidden * raw, axis=1, keepdims=True)
+            hid_grad = gate_col * raw
             gate_grad = hid_grad * u * logistic * (1.0 + g * (1.0 - logistic))
-            up_grad = hid_grad * swish
-            scaled_ref[m, rows, :] = (hidden * gate_row).astype(BF16)
-            ggt_ref[:, rows] = gate_grad.T.astype(BF16)
-            ugt_ref[:, rows] = up_grad.T.astype(BF16)
-        psend[m] = jnp.broadcast_to(prob, (16, width)).astype(BF16)
+            scaled_ref[m, :, rows] = (hidden * gate_col).astype(BF16)
+            ggt_ref[:, rows] = gate_grad.astype(BF16)
+            ugt_ref[:, rows] = (hid_grad * swish).astype(BF16)
+        psend[m] = jnp.broadcast_to(prob, (width, 128)).T[0:16].astype(BF16)
 
     def give_back(m, phase):
         def go(d):
             peer_copy(psend.at[m], precv.at[m, me], pssem.at[m, d], prsem.at[m, me], d).start()
 
         each_peer(go)
-
-        def body(c):
-            part = dot(ggt_ref[...], wg_ref[:, c]) + dot(ugt_ref[...], wu_ref[:, c])
-            for j in range(n):
-                sbuf[phase, j, :, c] = part[j * CAP : (j + 1) * CAP].astype(BF16)
-
-        tiles(dim, cols, body)
-        send_rows(phase, False)
-        rbuf[phase, me] = sbuf[phase, me]
+        for h in range(HALVES):
+
+            def body(c):
+                w = slice(h * part + c.start, h * part + c.stop)
+                total = dot(ggt_ref[...], wg_ref[:, w]) + dot(ugt_ref[...], wu_ref[:, w])
+                for j in range(n):
+                    sbuf[phase, h, j, :, c] = total[j * CAP : (j + 1) * CAP].astype(BF16)
+
+            half_tiles(body)
+            send_rows(phase, h, False)
+            rbuf[phase, h, me] = sbuf[phase, h, me]
         precv[m, me] = psend[m]
 
-    def combine(m, phase, info, src, dst):
+    def logits_back(m, info):
         def arrived(d):
             peer_copy(psend.at[m], precv.at[m, d], pssem.at[m, d], prsem.at[m, d], d).wait_recv()
 
@@ -205,18 +216,22 @@
         logit = info["z_term"]
         for k in range(TOP):
             logit = logit + info["named"][k] * (gates[k] * (probs[k] - mean))
-        logit = logit.astype(BF16)
-        wait_rows(phase)
+        return logit.astype(BF16)
+
+    def combine(phase, h, info, logit, src, store_to):
+        wait_rows(phase, h)
 
         def body(c):
-            total = src[:, c].astype(F32) + dot(info["gather"], joined(phase, c))
-            dst[:, c] = (total + dot(logit, wr_ref[:, c])).astype(BF16)
-
-        tiles(dim, cols, body)
+            w = slice(h * part + c.start, h * part + c.stop)
+            total = src[:, w].astype(F32) + dot(info["gather"], joined(phase, h, c))
+            store_to(h, c, w, (total + dot(logit, wr_ref[:, w])).astype(BF16))
+
+        half_tiles(body)
 
     first = route(0)
     pl.semaphore_wait(barrier, n + 1)
-    dispatch(D0, first["spread_t"], grad_ref)
+    for h in range(HALVES):
+        dispatch(D0, h, first["spread_t"], grad_ref)
     second = route(1)
     half = lax.broadcasted_iota(jnp.int32, (16, width), 0) < 8
     for d in range(n):
@@ -238,38 +253,58 @@
 
     for load in loads:
         load.wait()
-    wait_rows(D0)
-    local(0, D0, gate_all[0:1])
+    gate_cols = gate_all.T
+    local(0, D0, gate_cols[:, 0:1])
     give_back(0, R0)
-    combine(0, R0, first, grad_ref, hsend)
-    pass_on = pltpu.make_async_remote_copy(
-        src_ref=hsend, dst_ref=hrecv, send_sem=hsem.at[0], recv_sem=hsem.at[1],
-        device_id=(down, me), device_id_type=pl.DeviceIdType.MESH,
-    )
-    pass_on.start()
-    pass_on.wait_recv()
+    logit = logits_back(0, first)
+
+    def keep(h, c, w, value):
+        hsend[h, :, c] = value
+
+    def pass_on(h):
+        return pltpu.make_async_remote_copy(
+            src_ref=hsend.at[h], dst_ref=hrecv.at[h], send_sem=hsem.at[0, h], recv_sem=hsem.at[1, h],
+            device_id=(down, me), device_id_type=pl.DeviceIdType.MESH,
+        )
+
     is_last = pipe == pipes - 1
-    g1_ref[...] = jnp.where(is_last, head_ref[...], hrecv[...])
-    dispatch(D1, second["spread_t"], g1_ref)
-    wait_rows(D1)
-    local(1, D1, gate_all[8:9])
+    for h in range(HALVES):
+        combine(R0, h, first, logit, grad_ref, keep)
+        pass_on(h).start()
+    for h in range(HALVES):
+        pass_on(h).wait_recv()
+        w = slice(h * part, (h + 1) * part)
+        g1_ref[:, w] = jnp.where(is_last, head_ref[:, w], hrecv[h])
+        dispatch(D1, h, second["spread_t"], g1_ref)
+    local(1, D1, gate_cols[:, 8:9])
     give_back(1, R1)
 
+    for m in range(2):
+        st_ref[m] = scaled_ref[m].astype(F32).T.astype(BF16)
+
     def weigh(c):
-        total = dot(scaled_ref[0], x_ref[0, :, c]) + dot(scaled_ref[1], x_ref[1, :, c])
+        total = dot(st_ref[0], x_ref[0, :, c]) + dot(st_ref[1], x_ref[1, :, c])
         dgv[:, c] = total.astype(BF16)
 
     tiles(dim, 256 if dim % 256 == 0 else dim, weigh)
     store = pltpu.make_async_copy(dgv, dg_hbm, lsem.at[0])
     store.start()
-    combine(1, R1, second, g1_ref, out_ref)
+    logit = logits_back(1, second)
+
+    def write(h, c, w, value):
+        out_ref[:, w] = value
+
+    for h in range(HALVES):
+        combine(R1, h, second, logit, g1_ref, write)
     store.wait()
-    pass_on.wait_send()
+    for h in range(HALVES):
+        pass_on(h).wait_send()
 
     def drain(d):
         for phase in range(4):
-            src = sbuf.at[phase, d]
-            peer_copy(src, src, ssem.at[phase, d], rsem.at[phase, d], d).wait_send()
+            for h in range(HALVES):
+                src = sbuf.at[phase, h, d]
+                peer_copy(src, src, ssem.at[phase, h, d], rsem.at[phase, h, d], d).wait_send()
         for m in range(2):
             peer_copy(psend.at[m], precv.at[m, d], pssem.at[m, d], prsem.at[m, d], d).wait_send()
         peer_copy(gsend.at[d], grecv.at[d], gssem.at[d], grsem.at[d], d).wait_send()
@@ -299,26 +334,27 @@
         in_specs=[vmem, vmem, vmem, vmem, smem, vmem, hbm, hbm, hbm, hbm, hbm],
         out_specs=(vmem, hbm),
         scratch_shapes=[
-            pltpu.VMEM((4, n, CAP, dim), BF16),
-            pltpu.VMEM((4, n, CAP, dim), BF16),
+            pltpu.VMEM((4, HALVES, n, CAP, dim // HALVES), BF16),
+            pltpu.VMEM((4, HALVES, n, CAP, dim // HALVES), BF16),
             pltpu.VMEM((n, 16, width), BF16),
             pltpu.VMEM((n, 16, width), BF16),
             pltpu.VMEM((2, 16, width), BF16),
             pltpu.VMEM((2, n, 16, width), BF16),
-            pltpu.VMEM((tok, dim), BF16),
-            pltpu.VMEM((tok, dim), BF16),
+            pltpu.VMEM((HALVES, tok, dim // HALVES), BF16),
+            pltpu.VMEM((HALVES, tok, dim // HALVES), BF16),
             pltpu.VMEM((tok, dim), BF16),
             pltpu.VMEM((2, width, dim), BF16),
+            pltpu.VMEM((2, width, hid), BF16),
             pltpu.VMEM((2, hid, width), BF16),
             pltpu.VMEM((width, hid), BF16),
             pltpu.VMEM((width, hid), BF16),
             pltpu.VMEM((hid, dim), BF16),
-            pltpu.VMEM((2, hid, width), BF16),
-            pltpu.VMEM((2, hid, width), BF16),
+            pltpu.VMEM((2, width, hid), BF16),
+            pltpu.VMEM((2, width, hid), BF16),
             pltpu.VMEM((hid, dim), BF16),
             pltpu.VMEM((hid, dim), BF16),
             pltpu.VMEM((hid, dim), BF16),
-            dma((4, n)), dma((4, n)), dma((n,)), dma((n,)), dma((2, n)), dma((2, n)), dma((2,)), dma((5,)),
+            dma((4, HALVES, n)), dma((4, HALVES, n)), dma((n,)), dma((n,)), dma((2, n)), dma((2, n)), dma((2, HALVES)), dma((5,)),
         ],
         compiler_params=pltpu.CompilerParams(
             collective_id=0, has_side_effects=True, vmem_limit_bytes=56 * 1024 * 1024
@@ -327,8 +363,8 @@
             flops=16 * hid * width * dim, bytes_accessed=8 * hid * dim, transcendentals=2 * hid * width
         ),
     )(
-        grad_in[0], head_grad, router_logits[0], route_ids[0], z_weight.reshape(1, 1),
-        router_weight[0].T, gate_act[0], up_act[0], gate_weight[0], up_weight[0], down_weight[0],
+        grad_in[0], head_grad, jnp.swapaxes(router_logits[0], 1, 2), jnp.swapaxes(route_ids[0], 1, 2), z_weight.reshape(1, 1),
+        router_weight[0].T, jnp.swapaxes(gate_act[0], 1, 2), jnp.swapaxes(up_act[0], 1, 2), gate_weight[0], up_weight[0], down_weight[0],
     )
     return out[None], dg[None]
 

time: 108 us -> 96.4 us (0.89)
  the two profiles are of different devices: /device:TPU:19 before, /device:TPU:0 now
where the time goes in v2:
time: 96.4 us; the launch traced here: 96.1 us
  Pallas kernels  89.2 us (93%)
  local copies, waits for them, and re-layouts  5.64 us (6%)
  between operations  1.29 us (1%)
    pallas_call x1, Pallas kernels, per_device(): pl.pallas_call(functools.partial(kernel, n, pipes), out_shape=(jax.ShapeD...  89.2 us
    unnamed x2, local copies, waits for them, and re-layouts  5.64 us

profile of v2, /device:TPU:0, one launch (start us, length us, event | category | flops | bytes accessed | tf_op | source)
XLA Modules:
  0.0 96.1 jit_solution(2888780971166749148)
XLA Ops:
  1.3 89.2 %shard_map.122 = (bf16[64,2048]{1,0:T(8,128)(2,1)}, bf16[768,2048]{1,0:T(8,128)(2,1)}) custom-call(bf16[64,2048]{1,0:T(8,128)(2,1)} %bitcast.30, bf16[64,2048]{1,0:T(8,128)(2,1)} %head_ref.1, f32[2,8,64]{2,1,0:T(8,128)} %bitcast.32, s32[2,2,64]{2,1,0:T(2,128)} %bitcast.33, f32[1,1]{1,0:T(1,128)} %bitcast.22.zw_ref, bf16[8,2048]{1,0:T(8,128)(2,1)} %bitcast.31, ...), custom_call_target="tpu_custom_call" | custom-call | flops 4831838208 | bytes 12582912 | tf_op jit(solution)/shard_map/pallas_call | solution.py:328
  90.5 1.7 %copy.16 = bf16[1,64,2048]{2,1,0:T(8,128)(2,1)} copy(bf16[1,64,2048]{2,1,0:T(8,128)(2,1)} %bitcast.24) | data formatting | bytes 524288
  92.2 4.0 %copy.17 = bf16[1,768,2048]{2,1,0:T(8,128)(2,1)} copy(bf16[1,768,2048]{2,1,0:T(8,128)(2,1)} %bitcast.23) | data formatting | bytes 6291456

commit v3 on v2

--- a/solution.py
+++ b/solution.py
@@ -71,9 +71,9 @@
             device_id=(pipe, p), device_id_type=pl.DeviceIdType.MESH,
         )
 
-    def each_peer(body):
+    def each_peer(body, first_step=1):
         def step(p, carry):
-            body(lax.rem(me + p, n))
+            body(lax.rem(me + 1 + lax.rem(p + first_step + n - 3, n - 1), n))
             return carry
 
         lax.fori_loop(1, n, step, 0)
@@ -130,7 +130,7 @@
             src = sbuf.at[phase, h, d // slices if by_expert else d]
             peer_copy(src, rbuf.at[phase, h, me], ssem.at[phase, h, d], rsem.at[phase, h, me], d).start()
 
-        each_peer(go)
+        each_peer(go, n // 2 - 1)
 
     def wait_rows(phase, h):
         def go(d):

time: 96.4 us -> 95.9 us (level)
  no operation moved by 1% of the time
where the time goes in v3:
time: 95.9 us; the launch traced here: 95.2 us
  Pallas kernels  88.3 us (92%)
  local copies, waits for them, and re-layouts  5.64 us (6%)
  between operations  1.29 us (1%)
    pallas_call x1, Pallas kernels, per_device(): pl.pallas_call(functools.partial(kernel, n, pipes), out_shape=(jax.ShapeD...  88.3 us
    unnamed x2, local copies, waits for them, and re-layouts  5.64 us

profile of v3, /device:TPU:0, one launch (start us, length us, event | category | flops | bytes accessed | tf_op | source)
XLA Modules:
  0.0 95.2 jit_solution(5013167747962577377)
XLA Ops:
  1.3 88.3 %shard_map.122 = (bf16[64,2048]{1,0:T(8,128)(2,1)}, bf16[768,2048]{1,0:T(8,128)(2,1)}) custom-call(bf16[64,2048]{1,0:T(8,128)(2,1)} %bitcast.30, bf16[64,2048]{1,0:T(8,128)(2,1)} %head_ref.1, f32[2,8,64]{2,1,0:T(8,128)} %bitcast.32, s32[2,2,64]{2,1,0:T(2,128)} %bitcast.33, f32[1,1]{1,0:T(1,128)} %bitcast.22.zw_ref, bf16[8,2048]{1,0:T(8,128)(2,1)} %bitcast.31, ...), custom_call_target="tpu_custom_call" | custom-call | flops 4831838208 | bytes 12582912 | tf_op jit(solution)/shard_map/pallas_call | solution.py:328
  89.6 1.7 %copy.16 = bf16[1,64,2048]{2,1,0:T(8,128)(2,1)} copy(bf16[1,64,2048]{2,1,0:T(8,128)(2,1)} %bitcast.24) | data formatting | bytes 524288
  91.3 4.0 %copy.17 = bf16[1,768,2048]{2,1,0:T(8,128)(2,1)} copy(bf16[1,768,2048]{2,1,0:T(8,128)(2,1)} %bitcast.23) | data formatting | bytes 6291456

commit v4 on v3

--- a/solution.py
+++ b/solution.py
@@ -310,6 +310,23 @@
         peer_copy(gsend.at[d], grecv.at[d], gssem.at[d], grsem.at[d], d).wait_send()
 
     each_peer(drain)
+
+
+def hand_on(pieces, out_src, dg_src, out_dst, dg_dst, sems):
+    rows = dg_src.shape[0] // pieces
+    if rows % 16:
+        pieces, rows = 1, dg_src.shape[0]
+    copies = [
+        pltpu.make_async_copy(
+            dg_src.at[pl.ds(i * rows, rows)], dg_dst.at[pl.ds(i * rows, rows)], sems.at[i]
+        )
+        for i in range(pieces)
+    ]
+    copies.append(pltpu.make_async_copy(out_src, out_dst, sems.at[pieces]))
+    for copy in copies:
+        copy.start()
+    for copy in copies:
+        copy.wait()
 
 
 def per_device(
@@ -366,6 +383,18 @@
         grad_in[0], head_grad, jnp.swapaxes(router_logits[0], 1, 2), jnp.swapaxes(route_ids[0], 1, 2), z_weight.reshape(1, 1),
         router_weight[0].T, jnp.swapaxes(gate_act[0], 1, 2), jnp.swapaxes(up_act[0], 1, 2), gate_weight[0], up_weight[0], down_weight[0],
     )
+    pieces = 8
+    out, dg = pl.pallas_call(
+        functools.partial(hand_on, pieces),
+        out_shape=(
+            jax.ShapeDtypeStruct((tok, dim), BF16),
+            jax.ShapeDtypeStruct((hid, dim), BF16),
+        ),
+        in_specs=[hbm, hbm],
+        out_specs=(hbm, hbm),
+        scratch_shapes=[dma((pieces + 1,))],
+        cost_estimate=pl.CostEstimate(flops=0, bytes_accessed=4 * hid * dim, transcendentals=0),
+    )(out, dg)
     return out[None], dg[None]
 
 

time: 95.9 us -> 195 us (2.03)
  Pallas kernels: 88.3 us -> 193 us
  local copies, waits for them, and re-layouts: 5.64 us -> 0 us
    pallas_call x0 -> x1, Pallas kernels: none -> 104 us  [per_device(): pl.pallas_call(functools.partial(hand_on, pieces), out_shape=(jax.ShapeDt...]
    unnamed x2 -> x0, local copies, waits for them, and re-layouts: 5.64 us -> none
where the time goes in v4:
time: 195 us; the launch traced here: 194 us
  Pallas kernels  193 us (99%)
    pallas_call x1, Pallas kernels, per_device(): pl.pallas_call(functools.partial(hand_on, pieces), out_shape=(jax.ShapeDt...  104 us
    pallas_call x1, Pallas kernels, per_device(): pl.pallas_call(functools.partial(kernel, n, pipes), out_shape=(jax.ShapeD...  88.3 us

profile of v4, /device:TPU:0, one launch (start us, length us, event | category | flops | bytes accessed | tf_op | source)
XLA Modules:
  0.0 194.0 jit_solution(3471636885646293671)
XLA Ops:
  1.3 88.3 %shard_map.122 = (bf16[64,2048]{1,0:T(8,128)(2,1)}, bf16[768,2048]{1,0:T(8,128)(2,1)}) custom-call(bf16[64,2048]{1,0:T(8,128)(2,1)} %bitcast.29, bf16[64,2048]{1,0:T(8,128)(2,1)} %head_ref.1, f32[2,8,64]{2,1,0:T(8,128)} %bitcast.32, s32[2,2,64]{2,1,0:T(2,128)} %bitcast.33, f32[1,1]{1,0:T(1,128)} %bitcast.22.zw_ref, bf16[8,2048]{1,0:T(8,128)(2,1)} %bitcast.31, ...), custom_call_target="tpu_custom_call" | custom-call | flops 4831838208 | bytes 12582912 | tf_op jit(solution)/shard_map/pallas_call | solution.py:345
  89.6 104.4 %shard_map.123 = (bf16[64,2048]{1,0:T(8,128)(2,1)}, bf16[768,2048]{1,0:T(8,128)(2,1)}) custom-call(bf16[64,2048]{1,0:T(8,128)(2,1)} %get-tuple-element.6.out_src, bf16[768,2048]{1,0:T(8,128)(2,1)} %get-tuple-element.7.dg_src), custom_call_target="tpu_custom_call" | custom-call | bytes 6291456 | tf_op jit(solution)/shard_map/pallas_call | solution.py:387
